TPU v7x, 32 devices: a whole 2x2x4 slice. The times are simulated.
32 devices in a mesh: replica: 8 (over z, y), tensor: 4 (over x, core).
Axes of the slice: x: 2, y: 2, z: 4, core: 2. Of those that a mesh axis runs over, the one named last changes fastest.
Arguments:
- attended: bfloat16 [8192, 8192], P('replica', 'tensor'), may hold values from -6 to 6
- out_weight: bfloat16 [8192, 8192], P('tensor'), may hold values from -0.09375 to 0.09375
- shrink_weight: bfloat16 [96, 64, 8192], P('replica', None, 'tensor'), may hold values from -0.0625 to 0.0625
- expand_weight: bfloat16 [96, 64, 8192], P('replica', None, 'tensor'), may hold values from -0.75 to 0.75
- block_adapter: int32 [64], P('replica'), may hold values from 0 to 95, as said below
- block_fill: int32 [64], P('replica'), may hold values from 1 to 128
Outputs:
- projected: bfloat16 [8192, 8192], P('replica', 'tensor')
Inputs may be any that keep to these rules, and one draw needn't show every extreme that they name: `block_adapter`: the owner of adapter j is replica j // 12. Among the 8 blocks of one replica, at most 2 have adapters of one owner; one owner gets exactly 2 blocks from every replica.
All inputs are finite; a program needn't handle non-finite values.
Results may differ from a plain program's by a relative error of at most 0.02.
Values may be sent and summed in bfloat16 or wider, within the bound.
A program may use at most 128 MiB of HBM per device.

v0:
```python
import jax
import jax.numpy as jnp
from jax import lax
from jax.sharding import PartitionSpec as P


def slot_layout(block_ids, per_owner, capacity):
    block_owner = block_ids // per_owner
    local_ids = block_ids - block_owner * per_owner
    positions = jnp.arange(block_ids.shape[-1])
    earlier_same = (block_owner[..., None, :] == block_owner[..., :, None]) & (
        positions[None, :] < positions[:, None]
    )
    slot_rank = jnp.sum(earlier_same.astype(jnp.int32), axis=-1)
    return (block_owner * capacity + slot_rank, local_ids)


def local(attended, out_weight, shrink_weight, expand_weight, block_adapter, block_fill):
    tok_rows, feature_piece = attended.shape
    block_count = block_adapter.shape[0]
    block_rows = tok_rows // block_count
    owner_count = lax.axis_size("replica")
    capacity = max(1, (2 * block_count + owner_count - 1) // owner_count)
    per_owner = shrink_weight.shape[0]
    slot_count = owner_count * capacity
    slot_index, local_ids = slot_layout(block_adapter, per_owner, capacity)
    block_table = lax.all_gather(block_adapter, "replica", axis=0, tiled=True).reshape(
        owner_count, block_count
    )
    all_slots, all_local = slot_layout(block_table, per_owner, capacity)
    wanted_slot = lax.axis_index("replica") * capacity + jnp.arange(capacity)
    served_hit = all_slots[:, None, :] == wanted_slot[None, :, None]
    served_ids = jnp.sum(jnp.where(served_hit, all_local[:, None, :], 0), axis=-1)
    row_blocks = attended.reshape(block_count, block_rows, feature_piece)
    slot_match = jnp.arange(slot_count)[:, None] == slot_index[None, :]
    slot_source = jnp.sum(jnp.where(slot_match, jnp.arange(block_count)[None, :], 0), axis=1)
    slot_filled = jnp.any(slot_match, axis=1)
    outgoing = jnp.where(slot_filled[:, None, None], row_blocks[slot_source], 0)
    outgoing = outgoing.reshape(owner_count, capacity, block_rows, feature_piece)
    arrived = lax.all_to_all(outgoing, "replica", split_axis=0, concat_axis=0, tiled=True)
    partial_low = jnp.einsum(
        "scbp,scrp->scrb", arrived, shrink_weight[served_ids], preferred_element_type=jnp.float32
    )
    low_rank = lax.psum(partial_low.astype(jnp.bfloat16), "tensor")
    delta_slots = jnp.einsum(
        "scrb,scrp->scbp", low_rank, expand_weight[served_ids], preferred_element_type=jnp.float32
    ).astype(jnp.bfloat16)
    returned = lax.all_to_all(delta_slots, "replica", split_axis=0, concat_axis=0, tiled=True)
    delta_rows = returned.reshape(slot_count, block_rows, feature_piece)[slot_index]
    partial_out = jnp.dot(attended, out_weight, preferred_element_type=jnp.float32)
    base_out = lax.psum_scatter(
        partial_out.astype(jnp.bfloat16), "tensor", scatter_dimension=1, tiled=True
    ).astype(jnp.float32)
    combined = base_out.reshape(block_count, block_rows, feature_piece) + delta_rows.astype(
        jnp.float32
    )
    live_rows = jnp.arange(block_rows)[None, :] < block_fill[:, None]
    projected = jnp.where(live_rows[:, :, None], combined, 0.0).astype(jnp.bfloat16)
    return projected.reshape(tok_rows, feature_piece)


def solution(mesh):
    in_specs = (
        P("replica", "tensor"),
        P("tensor", None),
        P("replica", None, "tensor"),
        P("replica", None, "tensor"),
        P("replica"),
        P("replica"),
    )
    out_specs = P("replica", "tensor")
    return jax.shard_map(local, mesh=mesh, in_specs=in_specs, out_specs=out_specs, check_vma=False)
```

profile of v0, /device:TPU:14, one launch (start us, length us, event | category | flops | bytes accessed | tf_op | source)
XLA Modules:
  0.0 484.6 jit_solution(4428203050060665704)
XLA Ops:
  6.5 0.0 copy-start
  6.5 0.8 and_select_fusion
  7.4 0.2 convert_reduce_fusion.1
  7.5 0.7 compare_select_fusion.1
  8.2 0.1 select_reduce_fusion.1
  8.3 0.1 fusion.2
  8.4 0.1 broadcast_in_dim.78
  8.5 6.9 %gather_fusion.1 = bf16[16,128,2048]{2,1,0:T(8,128)(2,1)} fusion(bf16[8,128,2048]{2,1,0:T(8,128)(2,1)} %bitcast.28, s32[1024]{0:T(1024)S(1)} %pad_clamp_fusion.1), kind=kCustom, calls=%fused_computation.1 | custom fusion | bytes 16777280 | tf_op jit(solution)/shard_map/gather | solution.py:38
  15.4 7.2 %broadcast_select_fusion = bf16[8,2,128,2048]{3,2,1,0:T(8,128)(2,1)} fusion(bf16[8,2,128,2048]{3,2,1,0:T(8,128)(2,1)} %bitcast.25, pred[8,2]{1,0:T(8,128)(4,1)S(1)} %broadcast_in_dim.78), kind=kLoop, calls=%fused_computation.8 | loop fusion | flops 4194304 | bytes 16777232 | tf_op jit(solution)/shard_map/jit(_where)/select_n | solution.py:38
  22.6 0.0 copy-start.5
  22.6 0.0 copy-start.3
  22.6 6.3 %all-to-all-start = ((bf16[8,2,128,2048]{3,2,1,0:T(8,128)(2,1)}), bf16[8,2,128,2048]{3,2,1,0:T(8,128)(2,1)}, u32[]{:S(2)}, u32[]{:S(2)}) async-start(bf16[8,2,128,2048]{3,2,1,0:T(8,128)(2,1)} %broadcast_select_fusion), calls=%async_computation.1 | async-start | bytes 16777216 | tf_op jit(solution)/shard_map/all_to_all | solution.py:40
  28.9 0.0 all-reduce.3.cloned.1.call-start
  28.9 0.0 copy-done.5
  28.9 0.6 dynamic-slice
  30.1 0.0 copy-done.3
  30.2 0.2 dynamic-update-slice
  30.4 178.4 %all-reduce = s32[64]{0:T(128)S(1)} all-reduce(s32[64]{0:T(128)S(1)} %dynamic-update-slice), channel_id=1, replica_groups=mesh['replica'=8,'tensor'=4] {'replica'}, use_global_device_ids=true, to_apply=%add | all-reduce | flops 64 | bytes 512
  208.8 0.1 reshape.144
  208.9 0.3 convert_reduce_fusion
  209.2 0.2 select_reduce_fusion
  209.5 0.1 copy.9
  209.5 0.1 reshape.150
  209.6 0.0 copy-done
  209.6 2.8 gather_fusion
  212.5 0.0 all-to-all-done
  212.5 8.3 %convolution_convert_fusion.2 = bf16[8,2,64,128]{3,2,1,0:T(8,128)(2,1)} fusion(bf16[8,2,64,2048]{3,2,1,0:T(8,128)(2,1)} %bitcast.26, bf16[8,2,128,2048]{3,2,1,0:T(8,128)(2,1)} %all-to-all-done), kind=kOutput, calls=%fused_computation.10 | convolution fusion | flops 537001984 | bytes 12845056 | tf_op jit(solution)/shard_map/scbp,scrp->scrb/dot_general | solution.py:41
  220.8 0.0 all-reduce.3.cloned.1.call-update
  220.8 0.2 reduce-scatter.2.cloned.1.call-start
  221.1 41.8 %convolution_convert_fusion = bf16[1024,8192]{1,0:T(8,128)(2,1)} fusion(bf16[1024,2048]{1,0:T(8,128)(2,1)} %param.6, bf16[2048,8192]{1,0:T(8,128)(2,1)} %param.7), kind=kOutput, calls=%fused_computation.4 | convolution fusion | flops 34368126976 | bytes 54525952 | tf_op jit(solution)/shard_map/dot_general | solution.py:50
  262.9 0.0 copy-start.2
  262.9 0.0 reduce-scatter.2.cloned.1.call-update
  262.9 1.9 copy-done.2
  264.8 2.8 gather_fusion.2
  267.6 0.0 all-reduce.3.cloned.1.call-done
  267.6 9.7 %convolution_convert_fusion.1 = bf16[8,2,128,2048]{3,2,1,0:T(8,128)(2,1)} fusion(bf16[8,2,64,128]{3,2,1,0:T(8,128)(2,1)} %all-reduce.3.cloned.1.call-done, bf16[8,2,64,2048]{3,2,1,0:T(8,128)(2,1)} %bitcast.27), kind=kOutput, calls=%fused_computation.9 | convolution fusion | flops 541065216 | bytes 12845056 | tf_op jit(solution)/shard_map/scrb,scrp->scbp/dot_general | solution.py:45
  277.4 0.0 copy-start.4
  277.4 8.7 %all-to-all-start.1 = ((bf16[8,2,128,2048]{3,2,1,0:T(8,128)(2,1)}), bf16[8,2,128,2048]{3,2,1,0:T(8,128)(2,1)}, u32[]{:S(2)}, u32[]{:S(2)}) async-start(bf16[8,2,128,2048]{3,2,1,0:T(8,128)(2,1)} %convolution_convert_fusion.1), calls=%async_computation.2 | async-start | bytes 16777216 | tf_op jit(solution)/shard_map/all_to_all | solution.py:48
  286.1 0.0 copy-done.4
  286.1 0.1 fusion.3
  286.2 179.2 %all-to-all-done.1 = bf16[8,2,128,2048]{3,2,1,0:T(8,128)(2,1)} async-done(((bf16[8,2,128,2048]{3,2,1,0:T(8,128)(2,1)}), bf16[8,2,128,2048]{3,2,1,0:T(8,128)(2,1)}, u32[]{:S(2)}, u32[]{:S(2)}) %all-to-all-start.1) | async-done | bytes 8388640 | tf_op jit(solution)/shard_map/all_to_all | solution.py:48
  465.4 0.0 copy-start.1
  465.4 6.3 %gather_fusion.3 = bf16[8,128,2048]{2,1,0:T(8,128)(2,1)} fusion(bf16[16,128,2048]{2,1,0:T(8,128)(2,1)} %bitcast.9, s32[1024]{0:T(1024)S(1)} %pad_clamp_fusion), kind=kCustom, calls=%fused_computation.3 | custom fusion | bytes 8388640 | tf_op jit(solution)/shard_map/gather | solution.py:49
  471.7 0.0 reduce-scatter.2.cloned.1.call-done
  471.7 6.0 %fusion.1 = bf16[1024,2048]{1,0:T(8,128)(2,1)} fusion(bf16[1024,2048]{1,0:T(8,128)(2,1)} %reduce-scatter.2.cloned.1.call-done, bf16[8,128,2048]{2,1,0:T(8,128)(2,1)} %gather_fusion.3, pred[1024]{0:T(1024)(128)(4,1)S(1)} %fusion.3), kind=kLoop, calls=%fused_computation.7 | loop fusion | flops 10485760 | bytes 12583936 | tf_op jit(solution)/shard_map/convert_element_type | solution.py:58
  477.7 0.0 copy-done.1
  (10 shorter events, 0.1 us)
Async XLA Ops:
  6.5 203.1 %copy-start = (bf16[12,64,2048]{2,1,0:T(8,128)(2,1)S(1)}, bf16[12,64,2048]{2,1,0:T(8,128)(2,1)}, u32[]{:S(2)}) copy-start(bf16[12,64,2048]{2,1,0:T(8,128)(2,1)} %param.8) | copy-start | bytes 9437188
  22.6 6.3 %copy-start.5 = (u32[32]{0:T(128)S(1)}, u32[32]{0:T(128)}, u32[]{:S(2)}) copy-start(u32[32]{0:T(128)} %constant.46) | copy-start | bytes 388
  22.6 7.6 %copy-start.3 = (s32[8]{0:T(128)S(1)}, s32[8]{0:T(128)}, u32[]{:S(2)}) copy-start(s32[8]{0:T(128)} %param.10) | copy-start | bytes 100
  22.6 189.9 %all-to-all-start = ((bf16[8,2,128,2048]{3,2,1,0:T(8,128)(2,1)}), bf16[8,2,128,2048]{3,2,1,0:T(8,128)(2,1)}, u32[]{:S(2)}, u32[]{:S(2)}) async-start(bf16[8,2,128,2048]{3,2,1,0:T(8,128)(2,1)} %broadcast_select_fusion), calls=%async_computation.1 | async-start | bytes 16777216 | tf_op jit(solution)/shard_map/all_to_all | solution.py:40
  28.9 238.7 %all-reduce.3.cloned.1.call-start = ((), (), s32[]{:S(2)}) async-start(), calls=%async_computation.4 | async-start | bytes 524288 | tf_op jit(solution)/shard_map/psum | solution.py:44
  220.8 250.9 %reduce-scatter.2.cloned.1.call-start = ((), (), s32[]{:S(2)}) async-start(), calls=%async_computation.3 | async-start | bytes 20971520 | tf_op jit(solution)/shard_map/reduce_scatter | solution.py:51
  262.9 1.9 copy-start.2
  277.4 8.8 %copy-start.4 = (s32[8]{0:T(128)S(1)}, s32[8]{0:T(128)}, u32[]{:S(2)}) copy-start(s32[8]{0:T(128)} %param.11) | copy-start | bytes 100
  277.4 188.1 %all-to-all-start.1 = ((bf16[8,2,128,2048]{3,2,1,0:T(8,128)(2,1)}), bf16[8,2,128,2048]{3,2,1,0:T(8,128)(2,1)}, u32[]{:S(2)}, u32[]{:S(2)}) async-start(bf16[8,2,128,2048]{3,2,1,0:T(8,128)(2,1)} %convolution_convert_fusion.1), calls=%async_computation.2 | async-start | bytes 16777216 | tf_op jit(solution)/shard_map/all_to_all | solution.py:48
  465.4 12.3 %copy-start.1 = (bf16[12,64,2048]{2,1,0:T(8,128)(2,1)S(1)}, bf16[12,64,2048]{2,1,0:T(8,128)(2,1)}, u32[]{:S(2)}) copy-start(bf16[12,64,2048]{2,1,0:T(8,128)(2,1)} %param.8) | copy-start | bytes 9437188
Sparse Core Ops, SparseCore 0:
  221.0 32.7 all-reduce.2
  263.1 127.0 reduce-scatter.1
where the time goes:
time: 490 us; the launch traced here: 485 us
  waiting for transfers between devices  179 us (37%)
  blocking collectives  178 us (36%)
  matrix products  59.9 us (12%)
  local copies, waits for them, and re-layouts  21.9 us (4%)
  other arithmetic  15.7 us (3%)
  starting transfers between devices  15.3 us (3%)
  between operations  14.1 us (3%)
    all_to_all x1, waiting for transfers between devices, local(): lax.all_to_all(delta_slots, 'replica', split_axis=0, concat_axis=0, tiled...  179 us
    unnamed x1, blocking collectives  178 us
    dot_general x1, matrix products, local(): jnp.dot(attended, out_weight, preferred_element_type=jnp.float32)  41.8 us
  transfers between devices with their start and end apart: 4, of which 1 were waited for; matrix products, arithmetic and copies ran while one was open for 13% of the time, Pallas kernels for 0%

commit v1 on v0

--- a/solution.py
+++ b/solution.py
@@ -19,6 +19,7 @@
     tok_rows, feature_piece = attended.shape
     block_count = block_adapter.shape[0]
     block_rows = tok_rows // block_count
+    rank = shrink_weight.shape[1]
     owner_count = lax.axis_size("replica")
     capacity = max(1, (2 * block_count + owner_count - 1) // owner_count)
     per_owner = shrink_weight.shape[0]
@@ -31,26 +32,22 @@
     wanted_slot = lax.axis_index("replica") * capacity + jnp.arange(capacity)
     served_hit = all_slots[:, None, :] == wanted_slot[None, :, None]
     served_ids = jnp.sum(jnp.where(served_hit, all_local[:, None, :], 0), axis=-1)
-    row_blocks = attended.reshape(block_count, block_rows, feature_piece)
-    slot_match = jnp.arange(slot_count)[:, None] == slot_index[None, :]
-    slot_source = jnp.sum(jnp.where(slot_match, jnp.arange(block_count)[None, :], 0), axis=1)
-    slot_filled = jnp.any(slot_match, axis=1)
-    outgoing = jnp.where(slot_filled[:, None, None], row_blocks[slot_source], 0)
-    outgoing = outgoing.reshape(owner_count, capacity, block_rows, feature_piece)
-    arrived = lax.all_to_all(outgoing, "replica", split_axis=0, concat_axis=0, tiled=True)
-    partial_low = jnp.einsum(
-        "scbp,scrp->scrb", arrived, shrink_weight[served_ids], preferred_element_type=jnp.float32
-    )
-    low_rank = lax.psum(partial_low.astype(jnp.bfloat16), "tensor")
-    delta_slots = jnp.einsum(
-        "scrb,scrp->scbp", low_rank, expand_weight[served_ids], preferred_element_type=jnp.float32
-    ).astype(jnp.bfloat16)
-    returned = lax.all_to_all(delta_slots, "replica", split_axis=0, concat_axis=0, tiled=True)
-    delta_rows = returned.reshape(slot_count, block_rows, feature_piece)[slot_index]
+    both = jnp.concatenate([shrink_weight[served_ids], expand_weight[served_ids]], axis=2)
+    arrived = lax.all_to_all(both, "replica", split_axis=0, concat_axis=0, tiled=True)
+    arrived = arrived.reshape(slot_count, 2 * rank, feature_piece)
     partial_out = jnp.dot(attended, out_weight, preferred_element_type=jnp.float32)
     base_out = lax.psum_scatter(
         partial_out.astype(jnp.bfloat16), "tensor", scatter_dimension=1, tiled=True
     ).astype(jnp.float32)
+    row_blocks = attended.reshape(block_count, block_rows, feature_piece)
+    mine = arrived[slot_index]
+    partial_low = jnp.einsum(
+        "bcp,brp->bcr", row_blocks, mine[:, :rank], preferred_element_type=jnp.float32
+    )
+    low_rank = lax.psum(partial_low.astype(jnp.bfloat16), "tensor")
+    delta_rows = jnp.einsum(
+        "bcr,brp->bcp", low_rank, mine[:, rank:], preferred_element_type=jnp.float32
+    ).astype(jnp.bfloat16)
     combined = base_out.reshape(block_count, block_rows, feature_piece) + delta_rows.astype(
         jnp.float32
     )

time: 490 us -> 417 us (0.85)
  blocking collectives: 178 us -> 10.5 us
  waiting for transfers between devices: 179 us -> 303 us
  starting transfers between devices: 15.3 us -> 6.54 us
  matrix products: 59.9 us -> 53.2 us
  other arithmetic: 15.7 us -> 9.18 us
  local copies, waits for them, and re-layouts: 21.9 us -> 16.7 us
    unnamed x1, blocking collectives: 178 us -> 10.5 us
    reduce_scatter x1, waiting for transfers between devices: 0.01 us -> 127 us  [local(): lax.psum_scatter(partial_out.astype(jnp.bfloat16), 'tensor', scatter_dime...]
    all_to_all x2 -> x1, starting transfers between devices: 15.1 us -> 6.49 us  [local(): lax.all_to_all(both, 'replica', split_axis=0, concat_axis=0, tiled=True)]
    concatenate x0 -> x1, other arithmetic: none -> 8.34 us  [local(): jnp.concatenate([shrink_weight[served_ids], expand_weight[served_ids]], a...]
    select_n x3 -> x1, other arithmetic: 7.88 us -> 0.02 us  [local(): mine = arrived[slot_index]]
    gather x2 -> x1, local copies, waits for them, and re-layouts: 13.2 us -> 6.12 us  [local(): mine = arrived[slot_index]]
    dot_general x2, matrix products: 18.1 us -> 11.4 us  [the longest x1 6.35 us: local(): jnp.einsum('bcr,brp->bcp', low_rank, mine[:, rank:], preferred_element_ty...]
    convert_element_type x1 -> x0, other arithmetic: 5.99 us -> none  [local(): jnp.where(live_rows[:, :, None], combined, 0.0).astype(jnp.bfloat16)]
  transfers between devices with their start and end apart: 4 -> 3, of which waited for: 1 -> 2; matrix products, arithmetic and copies ran while one was open for 13% -> 10% of each run, Pallas kernels for 0% -> 0%
where the time goes in v1:
time: 417 us; the launch traced here: 414 us
  waiting for transfers between devices  303 us (73%)
  matrix products  53.2 us (13%)
  local copies, waits for them, and re-layouts  16.7 us (4%)
  between operations  14.1 us (3%)
  blocking collectives  10.5 us (3%)
  other arithmetic  9.18 us (2%)
  starting transfers between devices  6.54 us (2%)
    all_to_all x1, waiting for transfers between devices, local(): lax.all_to_all(both, 'replica', split_axis=0, concat_axis=0, tiled=True)  177 us
    reduce_scatter x1, waiting for transfers between devices, local(): lax.psum_scatter(partial_out.astype(jnp.bfloat16), 'tensor', scatter_dime...  127 us
    dot_general x1, matrix products, local(): jnp.dot(attended, out_weight, preferred_element_type=jnp.float32)  41.8 us
    unnamed x1, blocking collectives  10.5 us
  transfers between devices with their start and end apart: 3, of which 2 were waited for; matrix products, arithmetic and copies ran while one was open for 10% of the time, Pallas kernels for 0%

profile of v1, /device:TPU:14, one launch (start us, length us, event | category | flops | bytes accessed | tf_op | source)
XLA Modules:
  0.0 413.7 jit_solution(3681936354019676492)
XLA Ops:
  6.5 0.0 copy-start
  6.5 1.4 dynamic-slice
  8.6 0.9 dynamic-update-slice
  9.5 10.5 %all-reduce = s32[64]{0:T(128)S(1)} all-reduce(s32[64]{0:T(128)S(1)} %dynamic-update-slice), channel_id=1, replica_groups=mesh['replica'=8,'tensor'=4] {'replica'}, use_global_device_ids=true, to_apply=%add | all-reduce | flops 64 | bytes 512
  19.9 0.1 reshape.131
  20.0 0.3 convert_reduce_fusion
  20.4 0.2 select_reduce_fusion
  20.6 0.1 copy.9
  20.7 0.1 reshape.139
  20.8 0.0 copy-done
  20.8 2.8 gather_fusion.1
  23.6 4.6 %gather_fusion = bf16[16,64,2048]{2,1,0:T(8,128)(2,1)} fusion(bf16[12,64,2048]{2,1,0:T(8,128)(2,1)} %param.8, s32[1024]{0:T(1024)S(1)} %pad_clamp_fusion.1), kind=kCustom, calls=%fused_computation | custom fusion | bytes 8388672 | tf_op jit(solution)/shard_map/gather | solution.py:35
  28.2 8.3 %pad_maximum_fusion = bf16[8,2,128,2048]{3,2,1,0:T(8,128)(2,1)} fusion(bf16[8,2,64,2048]{3,2,1,0:T(8,128)(2,1)} %bitcast.18, bf16[8,2,64,2048]{3,2,1,0:T(8,128)(2,1)} %bitcast.19), kind=kLoop, calls=%fused_computation.4 | loop fusion | flops 16777216 | bytes 16777216 | tf_op jit(solution)/shard_map/concatenate | solution.py:35
  36.6 0.0 copy-start.2
  36.6 6.5 %all-to-all-start = ((bf16[8,2,128,2048]{3,2,1,0:T(8,128)(2,1)}), bf16[8,2,128,2048]{3,2,1,0:T(8,128)(2,1)}, u32[]{:S(2)}, u32[]{:S(2)}) async-start(bf16[8,2,128,2048]{3,2,1,0:T(8,128)(2,1)} %pad_maximum_fusion), calls=%async_computation.1 | async-start | bytes 16777216 | tf_op jit(solution)/shard_map/all_to_all | solution.py:36
  43.1 0.0 all-reduce.3.cloned.1.call-start
  43.1 0.0 copy-done.2
  43.1 0.2 convert_reduce_fusion.1
  43.3 176.9 %all-to-all-done = bf16[8,2,128,2048]{3,2,1,0:T(8,128)(2,1)} async-done(((bf16[8,2,128,2048]{3,2,1,0:T(8,128)(2,1)}), bf16[8,2,128,2048]{3,2,1,0:T(8,128)(2,1)}, u32[]{:S(2)}, u32[]{:S(2)}) %all-to-all-start) | async-done | bytes 8388640 | tf_op jit(solution)/shard_map/all_to_all | solution.py:36
  220.2 6.1 %gather_fusion.2 = bf16[8,128,2048]{2,1,0:T(8,128)(2,1)} fusion(bf16[16,128,2048]{2,1,0:T(8,128)(2,1)} %bitcast.5, s32[1024]{0:T(1024)S(1)} %pad_clamp_fusion), kind=kCustom, calls=%fused_computation.2 | custom fusion | bytes 8388640 | tf_op jit(solution)/shard_map/gather | solution.py:43
  226.3 5.0 %fusion.8 = bf16[8,128,64]{1,2,0:T(8,128)(2,1)} fusion(bf16[8,128,2048]{2,1,0:T(8,128)(2,1)} %bitcast.20, bf16[8,128,2048]{2,1,0:T(8,128)(2,1)} %gather_fusion.2), kind=kOutput, calls=%fused_computation.12 | convolution fusion | flops 268500992 | bytes 6422528 | tf_op jit(solution)/shard_map/bcp,brp->bcr/dot_general | solution.py:44
  231.4 0.0 all-reduce.3.cloned.1.call-update
  231.4 0.0 reduce-scatter.2.cloned.1.call-start
  231.5 41.8 %convolution_convert_fusion = bf16[1024,8192]{1,0:T(8,128)(2,1)} fusion(bf16[1024,2048]{1,0:T(8,128)(2,1)} %param.6, bf16[2048,8192]{1,0:T(8,128)(2,1)} %param.7), kind=kOutput, calls=%fused_computation.3 | convolution fusion | flops 34368126976 | bytes 54525952 | tf_op jit(solution)/shard_map/dot_general | solution.py:38
  273.3 0.0 copy-start.3
  273.3 0.0 reduce-scatter.2.cloned.1.call-update
  273.3 0.6 copy-done.3
  273.9 0.1 iota_compare_fusion.1
  274.0 0.0 all-reduce.3.cloned.1.call-done
  274.0 126.5 %reduce-scatter.2.cloned.1.call-done = bf16[1024,2048]{1,0:T(8,128)(2,1)} async-done(((bf16[1024,8192]{1,0:T(8,128)(2,1)}), bf16[1024,2048]{1,0:T(8,128)(2,1)}) %reduce-scatter.2.cloned.1.call-update) | async-done | bytes 4194320 | tf_op jit(solution)/shard_map/reduce_scatter | solution.py:39
  400.5 0.0 copy-start.1
  400.5 6.4 %fusion.1 = bf16[8,128,2048]{2,1,0:T(8,128)(2,1)} fusion(bf16[8,128,2048]{2,1,0:T(8,128)(2,1)} %bitcast.21, pred[8,128]{1,0:T(8,128)(4,1)S(1)} %iota_compare_fusion.1, bf16[8,128,64]{1,2,0:T(8,128)(2,1)} %all-reduce.3.cloned.1.call-done, bf16[8,128,2048]{2,1,0:T(8,128)(2,1)} %gather_fusion.2), kind=kOutput, calls=%fused_computation.7 | convolution fusion | flops 281018368 | bytes 10617856 | tf_op jit(solution)/shard_map/bcr,brp->bcp/dot_general | solution.py:48
  406.9 0.0 copy-done.1
  (10 shorter events, 0.1 us)
Async XLA Ops:
  6.5 14.2 %copy-start = (bf16[12,64,2048]{2,1,0:T(8,128)(2,1)S(1)}, bf16[12,64,2048]{2,1,0:T(8,128)(2,1)}, u32[]{:S(2)}) copy-start(bf16[12,64,2048]{2,1,0:T(8,128)(2,1)} %param.9) | copy-start | bytes 9437188
  36.6 6.5 %copy-start.2 = (s32[8]{0:T(128)S(1)}, s32[8]{0:T(128)}, u32[]{:S(2)}) copy-start(s32[8]{0:T(128)} %param.10) | copy-start | bytes 100
  36.6 183.7 %all-to-all-start = ((bf16[8,2,128,2048]{3,2,1,0:T(8,128)(2,1)}), bf16[8,2,128,2048]{3,2,1,0:T(8,128)(2,1)}, u32[]{:S(2)}, u32[]{:S(2)}) async-start(bf16[8,2,128,2048]{3,2,1,0:T(8,128)(2,1)} %pad_maximum_fusion), calls=%async_computation.1 | async-start | bytes 16777216 | tf_op jit(solution)/shard_map/all_to_all | solution.py:36
  43.1 231.0 %all-reduce.3.cloned.1.call-start = ((), (), s32[]{:S(2)}) async-start(), calls=%async_computation.3 | async-start | bytes 262144 | tf_op jit(solution)/shard_map/psum | solution.py:47
  231.4 169.1 %reduce-scatter.2.cloned.1.call-start = ((), (), s32[]{:S(2)}) async-start(), calls=%async_computation.2 | async-start | bytes 20971520 | tf_op jit(solution)/shard_map/reduce_scatter | solution.py:39
  273.3 0.7 copy-start.3
  400.5 6.4 %copy-start.1 = (bf16[12,64,2048]{2,1,0:T(8,128)(2,1)S(1)}, bf16[12,64,2048]{2,1,0:T(8,128)(2,1)}, u32[]{:S(2)}) copy-start(bf16[12,64,2048]{2,1,0:T(8,128)(2,1)} %param.9) | copy-start | bytes 9437188
Sparse Core Ops, SparseCore 0:
  231.5 32.3 all-reduce.2
  273.4 127.0 reduce-scatter.1

commit v2 on v1

v2 whole, which is shorter than its diff:
```python
import functools

import jax
import jax.numpy as jnp
from jax import lax
from jax.experimental import pallas as pl
from jax.experimental.pallas import tpu as pltpu
from jax.sharding import PartitionSpec as P

MESH = pl.DeviceIdType.MESH
CHUNK = 512
ROW_TILE = 256


def kernel(R, T, cap, per, att_h, w_h, shrink_h, expand_h, tabin, ids, fill, out_h,
           att, shrink, expand, wbuf, tabv, tabs, stage_a, stage_e, recv_a, recv_e,
           psend, recvc, recvx, own, lowsend, lowrecv, low,
           load_sem, w_sem, tab_ssem, tab_rsem, tabs_sem, a_ssem, a_rsem, e_ssem, e_rsem,
           p_ssem, c_rsem, x_ssem, x_rsem, l_ssem, l_rsem, o_sem):
    me = lax.axis_index("replica")
    t = lax.axis_index("tensor")
    rows, f = att.shape
    B = ids.shape[0]
    blk = rows // B
    X = T // 2
    xc, c = t // 2, t % 2
    Q = f // CHUNK
    S = X * Q
    core_peer = t + 1 - 2 * c

    def w_copy(i, which):
        xo = lax.rem(xc + 1 + i // Q, X)
        piece = 2 * xo + (1 - c if which == 0 else c)
        col = pl.multiple_of(piece * f + lax.rem(i, Q) * CHUNK, CHUNK)
        return pltpu.make_async_copy(w_h.at[:, pl.ds(col, CHUNK)], wbuf.at[which], w_sem.at[which])

    att_load = pltpu.make_async_copy(att_h, att, load_sem.at[0])
    shrink_load = pltpu.make_async_copy(shrink_h, shrink, load_sem.at[1])
    expand_load = pltpu.make_async_copy(expand_h, expand, load_sem.at[2])
    shrink_load.start()
    expand_load.start()
    att_load.start()
    w_copy(0, 0).start()
    w_copy(0, 1).start()

    barrier = pltpu.get_barrier_semaphore()
    for k in range(1, R):
        pl.semaphore_signal(barrier, inc=1, device_id={"replica": lax.rem(me + k, R)}, device_id_type=MESH)
    for k in range(1, T):
        pl.semaphore_signal(barrier, inc=1, device_id={"tensor": lax.rem(t + k, T)}, device_id_type=MESH)
    pl.semaphore_wait(barrier, R + T - 2)

    def tab_copy(k):
        return pltpu.make_async_remote_copy(
            src_ref=tabin, dst_ref=tabv.at[me], send_sem=tab_ssem.at[k], recv_sem=tab_rsem.at[k],
            device_id={"replica": lax.rem(me + k, R)}, device_id_type=MESH)

    def adapter_copy(k, stage, recv, ssem, rsem):
        dst = lax.rem(me + k, R)
        return pltpu.make_async_remote_copy(
            src_ref=stage.at[dst], dst_ref=recv.at[me], send_sem=ssem.at[k], recv_sem=rsem.at[k],
            device_id={"replica": dst}, device_id_type=MESH)

    @pl.loop(1, R)
    def _(k):
        tab_copy(k).start()

    tabv[me] = tabin[...]

    @pl.loop(1, R)
    def _(k):
        tab_copy(k).wait()

    tab_local = pltpu.make_async_copy(tabv, tabs, tabs_sem)
    tab_local.start()
    tab_local.wait()

    def served(dst):
        count = jnp.int32(0)
        found = [jnp.int32(0) for _ in range(cap)]
        for b in range(B):
            local_id = tabs[dst, 0, b] - me * per
            mine = (local_id >= 0) & (local_id < per)
            for s in range(cap):
                found[s] = jnp.where(mine & (count == s), local_id, found[s])
            count = count + jnp.where(mine, 1, 0)
        return found

    def send_adapters(source, stage, recv, ssem, rsem):
        @pl.loop(1, R)
        def _(k):
            dst = lax.rem(me + k, R)
            for s, local_id in enumerate(served(dst)):
                stage[dst, s] = source[local_id]
            adapter_copy(k, stage, recv, ssem, rsem).start()

        for s, local_id in enumerate(served(me)):
            recv[me, s] = source[local_id]

    shrink_load.wait()
    send_adapters(shrink, stage_a, recv_a, a_ssem, a_rsem)
    expand_load.wait()
    send_adapters(expand, stage_e, recv_e, e_ssem, e_rsem)
    att_load.wait()

    def core_copy(i):
        slot = lax.rem(i, 2)
        return pltpu.make_async_remote_copy(
            src_ref=psend.at[slot], dst_ref=recvc.at[i], send_sem=p_ssem.at[slot], recv_sem=c_rsem.at[i],
            device_id={"tensor": core_peer}, device_id_type=MESH)

    def chip_copy(i):
        xo = lax.rem(xc + 1 + i // Q, X)
        return pltpu.make_async_remote_copy(
            src_ref=recvc.at[i], dst_ref=recvx.at[i], send_sem=x_ssem.at[i], recv_sem=x_rsem.at[i],
            device_id={"tensor": 2 * xo + c}, device_id_type=MESH)

    def product(which, tile):
        r = pl.ds(pl.multiple_of(tile * ROW_TILE, ROW_TILE), ROW_TILE)
        return r, jnp.dot(att[r, :], wbuf[which], preferred_element_type=jnp.float32)

    def for_peer(i):
        slot = lax.rem(i, 2)
        w_copy(i, 0).wait()

        @pl.when(i >= 2)
        def _():
            core_copy(i - 2).wait_send()

        @pl.loop(0, rows // ROW_TILE)
        def _(tile):
            r, value = product(0, tile)
            psend[slot, r, :] = value.astype(jnp.bfloat16)

        core_copy(i).start()

        @pl.when(i + 1 < S)
        def _():
            w_copy(i + 1, 0).start()

        w_copy(i, 1).wait()

    @pl.loop(0, S - Q)
    def _(i):
        for_peer(i)
        core_copy(i).wait_recv()

        @pl.loop(0, rows // ROW_TILE)
        def _(tile):
            r, value = product(1, tile)
            recvc[i, r, :] = (value + recvc[i, r, :].astype(jnp.float32)).astype(jnp.bfloat16)

        chip_copy(i).start()
        w_copy(i + 1, 1).start()

    @pl.loop(S - Q, S)
    def _(i):
        for_peer(i)
        col = pl.ds(pl.multiple_of((i - (S - Q)) * CHUNK, CHUNK), CHUNK)

        @pl.loop(0, rows // ROW_TILE)
        def _(tile):
            r, value = product(1, tile)
            own[r, col] = value.astype(jnp.bfloat16)

        @pl.when(i + 1 < S)
        def _():
            w_copy(i + 1, 1).start()

    @pl.loop(S - 2, S)
    def _(i):
        core_copy(i).wait_send()

    def place(b):
        owner = ids[b] // per
        slot = jnp.int32(0)
        for e in range(B):
            slot = slot + jnp.where((e < b) & (ids[e] // per == owner), 1, 0)
        return owner, jnp.minimum(slot, cap - 1)

    def low_copy(k):
        return pltpu.make_async_remote_copy(
            src_ref=lowsend, dst_ref=lowrecv.at[k], send_sem=l_ssem.at[k], recv_sem=l_rsem.at[k],
            device_id={"tensor": lax.rem(t + k, T)}, device_id_type=MESH)

    @pl.loop(1, R)
    def _(k):
        adapter_copy(k, stage_a, recv_a, a_ssem, a_rsem).wait()

    @pl.loop(0, B)
    def _(b):
        owner, slot = place(b)
        x_b = att[pl.ds(pl.multiple_of(b * blk, blk), blk), :]
        lowsend[b] = lax.dot_general(
            recv_a[owner, slot], x_b, (((1,), (1,)), ((), ())), preferred_element_type=jnp.float32
        ).astype(jnp.bfloat16)

    @pl.loop(1, T)
    def _(k):
        low_copy(k).start()

    @pl.loop(1, T)
    def _(k):
        low_copy(k).wait()

    @pl.loop(0, B)
    def _(b):
        total = lowsend[b].astype(jnp.float32)
        for k in range(1, T):
            total = total + lowrecv[k, b].astype(jnp.float32)
        low[b] = total.astype(jnp.bfloat16)

    @pl.loop(S - Q, S)
    def _(i):
        core_copy(i).wait_recv()

    @pl.loop(0, S - Q)
    def _(i):
        chip_copy(i).wait()

    @pl.loop(1, R)
    def _(k):
        adapter_copy(k, stage_e, recv_e, e_ssem, e_rsem).wait()

    def out_copy(b):
        r = pl.ds(pl.multiple_of(b * blk, blk), blk)
        return pltpu.make_async_copy(own.at[r, :], out_h.at[r, :], o_sem.at[b])

    @pl.loop(0, B)
    def _(b):
        owner, slot = place(b)
        r = pl.ds(pl.multiple_of(b * blk, blk), blk)
        live = lax.broadcasted_iota(jnp.int32, (blk, CHUNK), 0) < fill[b]
        for q in range(Q):
            cols = slice(q * CHUNK, (q + 1) * CHUNK)
            delta = lax.dot_general(
                low[b], recv_e[owner, slot, :, cols], (((0,), (0,)), ((), ())),
                preferred_element_type=jnp.float32).astype(jnp.bfloat16).astype(jnp.float32)
            base = own[r, cols].astype(jnp.float32) + recvc[S - Q + q, r, :].astype(jnp.float32)
            for j in range(X - 1):
                base = base + recvx[j * Q + q, r, :].astype(jnp.float32)
            own[r, cols] = jnp.where(live, base + delta, 0.0).astype(jnp.bfloat16)
        out_copy(b).start()

    @pl.loop(0, B)
    def _(b):
        out_copy(b).wait()


def local(R, T, attended, out_weight, shrink_weight, expand_weight, block_adapter, block_fill):
    rows, f = attended.shape
    B = block_adapter.shape[0]
    per, rank, _ = shrink_weight.shape
    cap = max(1, (2 * B + R - 1) // R)
    X = T // 2
    Q = f // CHUNK
    S = X * Q
    blk = rows // B
    tabin = jnp.broadcast_to(jnp.pad(block_adapter, (0, 128 - B))[None, :], (8, 128))
    bf = jnp.bfloat16
    dma = pltpu.SemaphoreType.DMA
    any_spec = pl.BlockSpec(memory_space=pl.ANY)
    return pl.pallas_call(
        functools.partial(kernel, R, T, cap, per),
        out_shape=jax.ShapeDtypeStruct((rows, f), bf),
        in_specs=[any_spec] * 4 + [pl.BlockSpec(memory_space=pltpu.VMEM)]
        + [pl.BlockSpec(memory_space=pltpu.SMEM)] * 2,
        out_specs=any_spec,
        scratch_shapes=[
            pltpu.VMEM((rows, f), bf),
            pltpu.VMEM((per, rank, f), bf),
            pltpu.VMEM((per, rank, f), bf),
            pltpu.VMEM((2, f, CHUNK), bf),
            pltpu.VMEM((R, 8, 128), jnp.int32),
            pltpu.SMEM((R, 8, 128), jnp.int32),
            pltpu.VMEM((R, cap, rank, f), bf),
            pltpu.VMEM((R, cap, rank, f), bf),
            pltpu.VMEM((R, cap, rank, f), bf),
            pltpu.VMEM((R, cap, rank, f), bf),
            pltpu.VMEM((2, rows, CHUNK), bf),
            pltpu.VMEM((S, rows, CHUNK), bf),
            pltpu.VMEM((S - Q, rows, CHUNK), bf),
            pltpu.VMEM((rows, f), bf),
            pltpu.VMEM((B, rank, blk), bf),
            pltpu.VMEM((T, B, rank, blk), bf),
            pltpu.VMEM((B, rank, blk), bf),
            dma((3,)), dma((2,)), dma((R,)), dma((R,)), dma,
            dma((R,)), dma((R,)), dma((R,)), dma((R,)),
            dma((2,)), dma((S,)), dma((S - Q,)), dma((S - Q,)), dma((T,)), dma((T,)), dma((B,)),
        ],
        compiler_params=pltpu.CompilerParams(
            collective_id=0, has_side_effects=True, vmem_limit_bytes=60 * 1024 * 1024
        ),
    )(attended, out_weight, shrink_weight, expand_weight, tabin, block_adapter, block_fill)


def solution(mesh):
    in_specs = (
        P("replica", "tensor"),
        P("tensor", None),
        P("replica", None, "tensor"),
        P("replica", None, "tensor"),
        P("replica"),
        P("replica"),
    )
    body = functools.partial(local, mesh.shape["replica"], mesh.shape["tensor"])
    return jax.shard_map(
        body, mesh=mesh, in_specs=in_specs, out_specs=P("replica", "tensor"), check_vma=False
    )
```

time: 417 us -> 201 us (0.48)
  waiting for transfers between devices: 303 us -> 0 us
  Pallas kernels: 0 us -> 195 us
  matrix products: 53.2 us -> 0 us
  between operations: 14.1 us -> 0.01 us
  local copies, waits for them, and re-layouts: 16.7 us -> 6.04 us
  blocking collectives: 10.5 us -> 0 us
  other arithmetic: 9.18 us -> 0 us
  starting transfers between devices: 6.54 us -> 0 us
    pallas_call x0 -> x1, Pallas kernels: none -> 195 us  [local(): pl.pallas_call(functools.partial(kernel, R, T, cap, per), out_shape=jax.S...]
    all_to_all x1 -> x0, waiting for transfers between devices: 177 us -> none  [local(): lax.all_to_all(both, 'replica', split_axis=0, concat_axis=0, tiled=True)]
    reduce_scatter x1 -> x0, waiting for transfers between devices: 127 us -> none  [local(): lax.psum_scatter(partial_out.astype(jnp.bfloat16), 'tensor', scatter_dime...]
    dot_general x3 -> x0, matrix products: 53.2 us -> none  [the longest x1 41.8 us: local(): jnp.dot(attended, out_weight, preferred_element_type=jnp.float32)]
    gather x3 -> x0, local copies, waits for them, and re-layouts: 13.6 us -> none  [the longest x1 6.12 us: local(): mine = arrived[slot_index]]
    unnamed x1 -> x0, blocking collectives: 10.5 us -> none
    concatenate x1 -> x0, other arithmetic: 8.34 us -> none  [local(): jnp.concatenate([shrink_weight[served_ids], expand_weight[served_ids]], a...]
    all_to_all x1 -> x0, starting transfers between devices: 6.49 us -> none  [local(): lax.all_to_all(both, 'replica', split_axis=0, concat_axis=0, tiled=True)]
  transfers between devices with their start and end apart: 3 -> 0, of which waited for: 2 -> 0; matrix products, arithmetic and copies ran while one was open for 10% -> 0% of each run, Pallas kernels for 0% -> 0%
where the time goes in v2:
time: 201 us
  Pallas kernels  195 us (97%)
  local copies, waits for them, and re-layouts  6.04 us (3%)
    pallas_call x1, Pallas kernels, local(): pl.pallas_call(functools.partial(kernel, R, T, cap, per), out_shape=jax.S...  195 us
    unnamed x1, local copies, waits for them, and re-layouts  4.79 us

profile of v2, /device:TPU:14, one launch (start us, length us, event | category | flops | bytes accessed | tf_op | source)
XLA Modules:
  0.0 201.1 jit_solution(4761925612967323911)
XLA Ops:
  0.0 0.7 pad.4
  0.7 0.6 broadcast_in_dim.2.tabin
  1.3 195.0 %shard_map.64 = bf16[1024,2048]{1,0:T(8,128)(2,1)} custom-call(bf16[1024,2048]{1,0:T(8,128)(2,1)} %att_h.1, bf16[2048,8192]{1,0:T(8,128)(2,1)} %w_h.1, bf16[12,64,2048]{2,1,0:T(8,128)(2,1)} %shrink_h.1, bf16[12,64,2048]{2,1,0:T(8,128)(2,1)} %expand_h.1, s32[8,128]{1,0:T(8,128)} %broadcast_in_dim.2.tabin, s32[8]{0:T(128)} %ids.1, s32[8]{0:T(128)} %fill.1), custom_call_target="tpu_custom_call" | custom-call | tf_op jit(solution)/shard_map/pallas_call | solution.py:263
  196.3 4.8 %copy.8 = bf16[1024,2048]{1,0:T(8,128)(2,1)} copy(bf16[1024,2048]{1,0:T(8,128)(2,1)} %shard_map.64) | data formatting | bytes 8388608

commit v3 on v2

--- a/solution.py
+++ b/solution.py
@@ -9,11 +9,12 @@
 
 MESH = pl.DeviceIdType.MESH
 CHUNK = 512
+STRIDE = 5
 ROW_TILE = 256
 
 
-def kernel(R, T, cap, per, att_h, w_h, shrink_h, expand_h, tabin, ids, fill, out_h,
-           att, shrink, expand, wbuf, tabv, tabs, stage_a, stage_e, recv_a, recv_e,
+def kernel(R, T, cap, per, att_h, w_h, shrink_h, expand_h, ids, fill, out_h,
+           att, shrink, expand, wbuf, tabin, tabv, tabs, stage_a, stage_e, recv_a, recv_e,
            psend, recvc, recvx, own, lowsend, lowrecv, low,
            load_sem, w_sem, tab_ssem, tab_rsem, tabs_sem, a_ssem, a_rsem, e_ssem, e_rsem,
            p_ssem, c_rsem, x_ssem, x_rsem, l_ssem, l_rsem, o_sem):
@@ -43,6 +44,12 @@
     w_copy(0, 0).start()
     w_copy(0, 1).start()
 
+    lane = lax.broadcasted_iota(jnp.int32, (8, 128), 1)
+    table = jnp.zeros((8, 128), jnp.int32)
+    for b in range(B):
+        table = jnp.where(lane == b, ids[b], table)
+    tabin[...] = table
+
     barrier = pltpu.get_barrier_semaphore()
     for k in range(1, R):
         pl.semaphore_signal(barrier, inc=1, device_id={"replica": lax.rem(me + k, R)}, device_id_type=MESH)
@@ -56,7 +63,7 @@
             device_id={"replica": lax.rem(me + k, R)}, device_id_type=MESH)
 
     def adapter_copy(k, stage, recv, ssem, rsem):
-        dst = lax.rem(me + k, R)
+        dst = lax.rem(me + STRIDE * k, R)
         return pltpu.make_async_remote_copy(
             src_ref=stage.at[dst], dst_ref=recv.at[me], send_sem=ssem.at[k], recv_sem=rsem.at[k],
             device_id={"replica": dst}, device_id_type=MESH)
@@ -65,7 +72,7 @@
     def _(k):
         tab_copy(k).start()
 
-    tabv[me] = tabin[...]
+    tabv[me] = table
 
     @pl.loop(1, R)
     def _(k):
@@ -86,21 +93,20 @@
             count = count + jnp.where(mine, 1, 0)
         return found
 
-    def send_adapters(source, stage, recv, ssem, rsem):
+    def send_adapters(source, stage, recv, ssem, rsem, cols=slice(None)):
         @pl.loop(1, R)
         def _(k):
-            dst = lax.rem(me + k, R)
+            dst = lax.rem(me + STRIDE * k, R)
             for s, local_id in enumerate(served(dst)):
-                stage[dst, s] = source[local_id]
+                stage[dst, s] = source[local_id, :, cols]
             adapter_copy(k, stage, recv, ssem, rsem).start()
 
         for s, local_id in enumerate(served(me)):
-            recv[me, s] = source[local_id]
+            recv[me, s] = source[local_id, :, cols]
 
     shrink_load.wait()
     send_adapters(shrink, stage_a, recv_a, a_ssem, a_rsem)
     expand_load.wait()
-    send_adapters(expand, stage_e, recv_e, e_ssem, e_rsem)
     att_load.wait()
 
     def core_copy(i):
@@ -153,6 +159,13 @@
         chip_copy(i).start()
         w_copy(i + 1, 1).start()
 
+    def send_expand(q):
+        cols = slice(q * CHUNK, (q + 1) * CHUNK)
+        send_adapters(expand, stage_e[q], recv_e[q], e_ssem.at[q], e_rsem.at[q], cols)
+
+    for q in range(Q // 2):
+        send_expand(q)
+
     @pl.loop(S - Q, S)
     def _(i):
         for_peer(i)
@@ -170,6 +183,9 @@
     @pl.loop(S - 2, S)
     def _(i):
         core_copy(i).wait_send()
+
+    for q in range(Q // 2, Q):
+        send_expand(q)
 
     def place(b):
         owner = ids[b] // per
@@ -218,33 +234,34 @@
     def _(i):
         chip_copy(i).wait()
 
-    @pl.loop(1, R)
-    def _(k):
-        adapter_copy(k, stage_e, recv_e, e_ssem, e_rsem).wait()
-
-    def out_copy(b):
-        r = pl.ds(pl.multiple_of(b * blk, blk), blk)
-        return pltpu.make_async_copy(own.at[r, :], out_h.at[r, :], o_sem.at[b])
-
-    @pl.loop(0, B)
-    def _(b):
-        owner, slot = place(b)
-        r = pl.ds(pl.multiple_of(b * blk, blk), blk)
-        live = lax.broadcasted_iota(jnp.int32, (blk, CHUNK), 0) < fill[b]
-        for q in range(Q):
-            cols = slice(q * CHUNK, (q + 1) * CHUNK)
+    def out_copy(q):
+        cols = pl.ds(q * CHUNK, CHUNK)
+        return pltpu.make_async_copy(own.at[:, cols], out_h.at[:, cols], o_sem.at[q])
+
+    for q in range(Q):
+        cols = slice(q * CHUNK, (q + 1) * CHUNK)
+
+        @pl.loop(1, R)
+        def _(k):
+            adapter_copy(k, stage_e[q], recv_e[q], e_ssem.at[q], e_rsem.at[q]).wait()
+
+        @pl.loop(0, B)
+        def _(b):
+            owner, slot = place(b)
+            r = pl.ds(pl.multiple_of(b * blk, blk), blk)
+            live = lax.broadcasted_iota(jnp.int32, (blk, CHUNK), 0) < fill[b]
             delta = lax.dot_general(
-                low[b], recv_e[owner, slot, :, cols], (((0,), (0,)), ((), ())),
+                low[b], recv_e[q][owner, slot], (((0,), (0,)), ((), ())),
                 preferred_element_type=jnp.float32).astype(jnp.bfloat16).astype(jnp.float32)
             base = own[r, cols].astype(jnp.float32) + recvc[S - Q + q, r, :].astype(jnp.float32)
             for j in range(X - 1):
                 base = base + recvx[j * Q + q, r, :].astype(jnp.float32)
             own[r, cols] = jnp.where(live, base + delta, 0.0).astype(jnp.bfloat16)
-        out_copy(b).start()
-
-    @pl.loop(0, B)
-    def _(b):
-        out_copy(b).wait()
+
+        out_copy(q).start()
+
+    for q in range(Q):
+        out_copy(q).wait()
 
 
 def local(R, T, attended, out_weight, shrink_weight, expand_weight, block_adapter, block_fill):
@@ -256,27 +273,26 @@
     Q = f // CHUNK
     S = X * Q
     blk = rows // B
-    tabin = jnp.broadcast_to(jnp.pad(block_adapter, (0, 128 - B))[None, :], (8, 128))
     bf = jnp.bfloat16
     dma = pltpu.SemaphoreType.DMA
     any_spec = pl.BlockSpec(memory_space=pl.ANY)
     return pl.pallas_call(
         functools.partial(kernel, R, T, cap, per),
         out_shape=jax.ShapeDtypeStruct((rows, f), bf),
-        in_specs=[any_spec] * 4 + [pl.BlockSpec(memory_space=pltpu.VMEM)]
-        + [pl.BlockSpec(memory_space=pltpu.SMEM)] * 2,
+        in_specs=[any_spec] * 4 + [pl.BlockSpec(memory_space=pltpu.SMEM)] * 2,
         out_specs=any_spec,
         scratch_shapes=[
             pltpu.VMEM((rows, f), bf),
             pltpu.VMEM((per, rank, f), bf),
             pltpu.VMEM((per, rank, f), bf),
             pltpu.VMEM((2, f, CHUNK), bf),
+            pltpu.VMEM((8, 128), jnp.int32),
             pltpu.VMEM((R, 8, 128), jnp.int32),
             pltpu.SMEM((R, 8, 128), jnp.int32),
             pltpu.VMEM((R, cap, rank, f), bf),
+            [pltpu.VMEM((R, cap, rank, CHUNK), bf) for _ in range(Q)],
             pltpu.VMEM((R, cap, rank, f), bf),
-            pltpu.VMEM((R, cap, rank, f), bf),
-            pltpu.VMEM((R, cap, rank, f), bf),
+            [pltpu.VMEM((R, cap, rank, CHUNK), bf) for _ in range(Q)],
             pltpu.VMEM((2, rows, CHUNK), bf),
             pltpu.VMEM((S, rows, CHUNK), bf),
             pltpu.VMEM((S - Q, rows, CHUNK), bf),
@@ -285,13 +301,13 @@
             pltpu.VMEM((T, B, rank, blk), bf),
             pltpu.VMEM((B, rank, blk), bf),
             dma((3,)), dma((2,)), dma((R,)), dma((R,)), dma,
-            dma((R,)), dma((R,)), dma((R,)), dma((R,)),
-            dma((2,)), dma((S,)), dma((S - Q,)), dma((S - Q,)), dma((T,)), dma((T,)), dma((B,)),
+            dma((R,)), dma((R,)), dma((Q, R)), dma((Q, R)),
+            dma((2,)), dma((S,)), dma((S - Q,)), dma((S - Q,)), dma((T,)), dma((T,)), dma((Q,)),
         ],
         compiler_params=pltpu.CompilerParams(
             collective_id=0, has_side_effects=True, vmem_limit_bytes=60 * 1024 * 1024
         ),
-    )(attended, out_weight, shrink_weight, expand_weight, tabin, block_adapter, block_fill)
+    )(attended, out_weight, shrink_weight, expand_weight, block_adapter, block_fill)
 
 
 def solution(mesh):

time: 201 us -> 202 us (level)
  the two profiles are of different devices: /device:TPU:14 before, /device:TPU:0 now
where the time goes in v3:
time: 202 us
  Pallas kernels  197 us (98%)
  local copies, waits for them, and re-layouts  4.79 us (2%)
    pallas_call x1, Pallas kernels, local(): pl.pallas_call(functools.partial(kernel, R, T, cap, per), out_shape=jax.S...  197 us
    unnamed x1, local copies, waits for them, and re-layouts  4.79 us

profile of v3, /device:TPU:0, one launch (start us, length us, event | category | flops | bytes accessed | tf_op | source)
XLA Modules:
  0.0 201.7 jit_solution(17547142892810012807)
XLA Ops:
  0.0 196.9 %shard_map.64 = bf16[1024,2048]{1,0:T(8,128)(2,1)} custom-call(bf16[1024,2048]{1,0:T(8,128)(2,1)} %att_h.1, bf16[2048,8192]{1,0:T(8,128)(2,1)} %w_h.1, bf16[12,64,2048]{2,1,0:T(8,128)(2,1)} %shrink_h.1, bf16[12,64,2048]{2,1,0:T(8,128)(2,1)} %expand_h.1, s32[8]{0:T(128)} %ids.1, s32[8]{0:T(128)} %fill.1), custom_call_target="tpu_custom_call" | custom-call | tf_op jit(solution)/shard_map/pallas_call | solution.py:279
  196.9 4.8 %copy.8 = bf16[1024,2048]{1,0:T(8,128)(2,1)} copy(bf16[1024,2048]{1,0:T(8,128)(2,1)} %shard_map.64) | data formatting | bytes 8388608

commit v4 on v3

--- a/solution.py
+++ b/solution.py
@@ -9,7 +9,7 @@
 
 MESH = pl.DeviceIdType.MESH
 CHUNK = 512
-STRIDE = 5
+STRIDE = 1
 ROW_TILE = 256
 
 

time: 202 us -> 199 us (0.985)
  the two profiles are of different devices: /device:TPU:0 before, /device:TPU:14 now
where the time goes in v4:
time: 199 us
  Pallas kernels  194 us (97%)
  local copies, waits for them, and re-layouts  4.79 us (2%)
    pallas_call x1, Pallas kernels, local(): pl.pallas_call(functools.partial(kernel, R, T, cap, per), out_shape=jax.S...  194 us
    unnamed x1, local copies, waits for them, and re-layouts  4.79 us

profile of v4, /device:TPU:14, one launch (start us, length us, event | category | flops | bytes accessed | tf_op | source)
XLA Modules:
  0.0 198.9 jit_solution(18074473499378676413)
XLA Ops:
  0.0 194.1 %shard_map.64 = bf16[1024,2048]{1,0:T(8,128)(2,1)} custom-call(bf16[1024,2048]{1,0:T(8,128)(2,1)} %att_h.1, bf16[2048,8192]{1,0:T(8,128)(2,1)} %w_h.1, bf16[12,64,2048]{2,1,0:T(8,128)(2,1)} %shrink_h.1, bf16[12,64,2048]{2,1,0:T(8,128)(2,1)} %expand_h.1, s32[8]{0:T(128)} %ids.1, s32[8]{0:T(128)} %fill.1), custom_call_target="tpu_custom_call" | custom-call | tf_op jit(solution)/shard_map/pallas_call | solution.py:279
  194.2 4.8 %copy.8 = bf16[1024,2048]{1,0:T(8,128)(2,1)} copy(bf16[1024,2048]{1,0:T(8,128)(2,1)} %shard_map.64) | data formatting | bytes 8388608
